TPU v7x, 256 devices: a whole 4x4x8 slice. The times are simulated.
256 devices in a mesh: noise: 8 (over z), row: 16 (over y, x), col: 2 (over core).
Axes of the slice: x: 4, y: 4, z: 8, core: 2. Of those that a mesh axis runs over, the one named last changes fastest.
Arguments:
- images: bfloat16 [256, 4, 6144], P('row', None, 'col'), may hold values from -40 to 40
- gain: float32 [6144], P('col'), may hold values from 0.3 to 3.5
- up_weight: bfloat16 [6144, 12288], P('col', 'row'), may hold values from -0.078125 to 0.078125
- down_weight: bfloat16 [12288, 6144], P('row', 'col'), may hold values from -0.0546875 to 0.0546875
- cotangent: bfloat16 [256, 16, 6144], P('row', 'noise', 'col'), may hold values from -6 to 6
- seeds: int32 [16], P('noise'), may hold values from 0 to 999999
- assign: int32 [16, 1], replicated, may hold values from 0 to 3, as said below
Outputs:
- saliency: float32 [256, 4, 6144], P('row', None, 'col')
Inputs may be any that keep to these rules, and one draw needn't show every extreme that they name: `assign`: every one of the 4 images is named by at least one copy.
All inputs are finite; a program needn't handle non-finite values.
Results may differ from a plain program's by a relative error of at most 0.0019.
Values may be sent and summed in bfloat16 or wider, within the bound.
A program may use at most 64 MiB of HBM per device.

v0:
```python
import math
import jax
import jax.numpy as jnp
from jax import lax
from jax.sharding import PartitionSpec as P

D = 6144
noise_scale = 0.6
gelu_coef = 0.044715
root_term = math.sqrt(2.0 / math.pi)


def mix_noise(seed_value, token_index, feature_index, width):
    linear = token_index[:, None] * width + feature_index[None, :]
    mixed = linear * 1664525 + seed_value * 1013904223
    mixed = mixed ^ mixed >> 13
    mixed = mixed * 1274126177
    mixed = mixed ^ mixed >> 16
    return ((mixed & 65535).astype(jnp.float32) - 32767.5) * (1.0 / 18918.0)


def gelu_slope(preact):
    inner = root_term * (preact + gelu_coef * preact * preact * preact)
    tanh_val = jnp.tanh(inner)
    return 0.5 * (1.0 + tanh_val) + 0.5 * preact * (1.0 - tanh_val * tanh_val) * root_term * (
        1.0 + 3.0 * gelu_coef * preact * preact
    )


def body(images, gain, up_weight, down_weight, cotangent, seeds, assign):
    tok_local = images.shape[0]
    image_count = images.shape[1]
    width_local = images.shape[2]
    planes = lax.axis_size("noise")
    rows = lax.axis_size("row")
    part = tok_local // planes
    col_index = lax.axis_index("col")
    row_index = lax.axis_index("row")
    noise_index = lax.axis_index("noise")
    all_seeds = lax.all_gather(seeds, "noise", tiled=True)
    slots = all_seeds.shape[0]
    own_cot = lax.all_to_all(cotangent, "noise", split_axis=0, concat_axis=1, tiled=True)
    own_images = lax.dynamic_slice_in_dim(images, noise_index * part, part)
    plane_images = lax.all_gather(own_images, "row", axis=0, tiled=True)
    plane_cot = lax.all_gather(own_cot, "row", axis=0, tiled=True)
    image_ids = jnp.arange(image_count, dtype=jnp.int32)
    onehot = (assign[:, 0][:, None] == image_ids[None, :]).astype(jnp.float32)
    counts = jnp.sum(onehot, axis=0)
    clean = jnp.einsum(
        "si,tid->tsd", onehot.astype(jnp.bfloat16), plane_images, preferred_element_type=jnp.float32
    )
    tokens = (
        jnp.arange(rows, dtype=jnp.int32)[:, None] * tok_local
        + noise_index * part
        + jnp.arange(part, dtype=jnp.int32)[None, :]
    ).reshape(-1)
    feature_index = col_index * width_local + jnp.arange(width_local, dtype=jnp.int32)
    noise_field = jax.vmap(
        lambda seed_value: mix_noise(seed_value, tokens, feature_index, D), out_axes=1
    )(all_seeds)
    noisy = clean + noise_scale * noise_field
    feat_mean = lax.psum(jnp.sum(noisy, axis=-1), "col") / D
    centred = noisy - feat_mean[..., None]
    feat_var = lax.psum(jnp.sum(centred * centred, axis=-1), "col") / D
    inv_std = lax.rsqrt(feat_var + 1e-06)
    normed = centred * inv_std[..., None]
    scaled = (normed * gain).astype(jnp.bfloat16)
    n = tokens.shape[0] * slots
    preact_part = jnp.dot(
        scaled.reshape(n, width_local), up_weight, preferred_element_type=jnp.float32
    )
    back_part = jnp.einsum(
        "td,hd->th",
        plane_cot.reshape(n, width_local),
        down_weight,
        preferred_element_type=jnp.float32,
    )
    ug_part = jnp.sum(gain[:, None] * up_weight.astype(jnp.float32), axis=0)
    preact, back_grad, ug = lax.psum((preact_part, back_part, ug_part), "col")
    hidden_grad = (back_grad * gelu_slope(preact)).astype(jnp.bfloat16)
    hg = hidden_grad.astype(jnp.float32)
    sums = jnp.stack([jnp.sum(hg * ug, axis=-1), jnp.sum(hg * preact, axis=-1)], axis=-1) / D
    sums = lax.psum_scatter(sums.reshape(-1, slots, 2), "row", scatter_dimension=0, tiled=True)
    weighted = jnp.einsum(
        "ts,si,tsh->tih",
        inv_std,
        onehot,
        hg.reshape(-1, slots, hg.shape[-1]),
        precision=lax.Precision.HIGHEST,
    ).astype(jnp.bfloat16)
    grad = jnp.einsum(
        "th,dh->td",
        weighted.reshape(-1, hg.shape[-1]),
        up_weight,
        preferred_element_type=jnp.float32,
    )
    grad = lax.psum_scatter(
        grad.reshape(-1, image_count, width_local), "row", scatter_dimension=0, tiled=True
    )
    own_normed = lax.dynamic_slice_in_dim(normed, row_index * part, part)
    own_inv = lax.dynamic_slice_in_dim(inv_std, row_index * part, part)
    rest = own_cot.astype(jnp.float32) - own_inv[..., None] * (
        sums[..., 0][..., None] + own_normed * sums[..., 1][..., None]
    )
    total = grad * gain + jnp.einsum("si,tsd->tid", onehot, rest, precision=lax.Precision.HIGHEST)
    total = total / counts[None, :, None]
    return lax.all_gather(total, "noise", axis=0, tiled=True)


def solution(mesh):
    placed = (
        P("row", None, "col"),
        P("col"),
        P("col", "row"),
        P("row", "col"),
        P("row", "noise", "col"),
        P("noise"),
        P(),
    )
    return jax.shard_map(
        body, mesh=mesh, in_specs=placed, out_specs=P("row", None, "col"), check_vma=False
    )
```

profile of v0, /device:TPU:2, one launch (start us, length us, event | category | flops | bytes accessed | tf_op | source)
XLA Modules:
  0.0 281.2 jit_solution(14509511110187522334)
XLA Ops:
  6.5 19.1 %all_to_all.18 = bf16[16,2,3072]{2,1,0:T(2,128)(2,1)S(1)} all-to-all(bf16[16,2,3072]{2,1,0:T(2,128)(2,1)} %param.11), channel_id=1, replica_groups=mesh['noise'=8,'row'=16,'col'=2] {'noise'}, dimensions={0} | all-to-all | bytes 393216 | tf_op jit(solution)/shard_map/all_to_all | solution.py:42
  25.6 0.1 copy.26
  25.7 0.8 all_to_all.16
  26.7 0.1 mul.175
  26.8 1.3 dynamic-slice
  28.8 0.9 dynamic-update-slice
  29.7 10.1 %all-reduce = s32[16]{0:T(128)S(1)} all-reduce(s32[16]{0:T(128)S(1)} %dynamic-update-slice), channel_id=1, replica_groups=mesh['noise'=8,'row'=16,'col'=2] {'noise'}, use_global_device_ids=true, to_apply=%add | all-reduce | flops 16 | bytes 128
  39.8 25.4 %all_gather.12 = bf16[32,4,3072]{2,1,0:T(4,128)(2,1)S(1)} all-gather(bf16[2,4,3072]{2,1,0:T(4,128)(2,1)S(1)} %constant_dynamic-slice_fusion.1), channel_id=1, replica_groups=mesh['noise'=8,'row'=16,'col'=2] {'row'}, dimensions={0}, use_global_device_ids=true | all-gather | bytes 835584 | tf_op jit(solution)/shard_map/all_gather | solution.py:44
  65.2 0.1 add_multiply_fusion
  65.3 5.3 %fusion.44 = (f32[32,16]{1,0:T(8,128)S(1)}, f32[32,16,3072]{2,1,0:T(8,128)}) fusion(s32[16]{0:T(128)S(1)} %broadcast_multiply_fusion.1, s32[32,3072]{1,0:T(8,128)S(1)} %add_multiply_fusion, bf16[32,4,3072]{2,1,0:T(4,128)(2,1)S(1)} %all_gather.12, s32[16]{0:T(128)} %bitcast.49), kind=kOutput, calls=%fused_computation.68 | convolution fusion | flops 31456960 | bytes 7473280 | tf_op jit(solution)/shard_map/si,tid->tsd/dot_general | solution.py:49
  70.7 3.5 %psum.35 = f32[32,16]{1,0:T(8,128)S(1)} all-reduce(f32[32,16]{1,0:T(8,128)S(1)} %get-tuple-element.18), channel_id=1, replica_groups=mesh['noise'=8,'row'=16,'col'=2] {'col'}, use_global_device_ids=true, to_apply=%region_1.0 | all-reduce | flops 512 | bytes 4096 | tf_op jit(solution)/shard_map/psum | solution.py:62
  74.1 3.5 %multiply_reduce_fusion.1 = f32[32,16]{1,0:T(8,128)S(1)} fusion(f32[32,16,3072]{2,1,0:T(8,128)} %get-tuple-element.19, f32[32,16]{1,0:T(8,128)S(1)} %broadcast_multiply_fusion), kind=kLoop, calls=%fused_computation.10 | loop fusion | flops 4718080 | bytes 6295552 | tf_op jit(solution)/shard_map/reduce_sum | solution.py:64
  77.7 3.4 %multiply_reduce_fusion = f32[768]{0:T(1024)S(1)} fusion(bf16[3072,768]{1,0:T(8,128)(2,1)} %param.9, f32[3072]{0:T(1024)S(1)} %copy-done.2), kind=kLoop, calls=%fused_computation.2 | loop fusion | flops 7077120 | bytes 4733952 | tf_op jit(solution)/shard_map/reduce_sum | solution.py:78
  81.1 3.6 %all-reduce.3 = (f32[32,16]{1,0:T(8,128)S(1)}, f32[768]{0:T(1024)S(1)}) all-reduce(f32[32,16]{1,0:T(8,128)S(1)} %multiply_reduce_fusion.1, f32[768]{0:T(1024)S(1)} %multiply_reduce_fusion), channel_id=1, replica_groups=mesh['noise'=8,'row'=16,'col'=2] {'col'}, use_global_device_ids=true, to_apply=%region_3.0 | all-reduce | flops 1280 | bytes 10240 | tf_op jit(solution)/shard_map/psum | solution.py:64
  84.7 7.3 %multiply_convert_fusion = (bf16[32,16,3072]{2,1,0:T(8,128)(2,1)S(1)}, f32[32,16,3072]{2,1,0:T(8,128)}) fusion(f32[3072]{0:T(1024)S(1)} %copy-done.2, f32[32,16]{1,0:T(8,128)S(1)} %get-tuple-element.17, f32[32,16,3072]{2,1,0:T(8,128)} %get-tuple-element.19, f32[32,16]{1,0:T(8,128)S(1)} %broadcast_multiply_fusion), kind=kLoop, calls=%fused_computation.9 | loop fusion | flops 6291456 | bytes 15745024 | tf_op jit(solution)/shard_map/convert_element_type | solution.py:67
  92.0 3.8 %fusion.46 = f32[512,768]{1,0:T(8,128)} fusion(bf16[512,3072]{1,0:T(8,128)(2,1)S(1)} %bitcast.46, bf16[3072,768]{1,0:T(8,128)(2,1)S(1)} %bitcast.44), kind=kOutput, calls=%fused_computation.70 | convolution fusion | flops 2415919104 | bytes 9437184 | tf_op jit(solution)/shard_map/dot_general | solution.py:69
  95.8 7.1 %fusion.45 = f32[512,768]{1,0:T(8,128)} fusion(bf16[512,3072]{1,0:T(8,128)(2,1)} %bitcast.53, bf16[768,3072]{1,0:T(8,128)(2,1)} %param.10), kind=kOutput, calls=%fused_computation.69 | convolution fusion | flops 2415919104 | bytes 9437184 | tf_op jit(solution)/shard_map/td,hd->th/dot_general | solution.py:72
  102.9 0.2 all-reduce.8.cloned.1.call-start
  103.2 31.5 %all-reduce.10.cloned.1.call-done = (f32[512,768]{1,0:T(8,128)}, f32[512,768]{1,0:T(8,128)}) async-done(((f32[512,768]{1,0:T(8,128)}, f32[512,768]{1,0:T(8,128)}), (f32[512,768]{1,0:T(8,128)}, f32[512,768]{1,0:T(8,128)})) %all-reduce.10.cloned.1.call-update) | async-done | bytes 3145744 | tf_op jit(solution)/shard_map/psum | solution.py:79
  134.7 3.2 %fusion.10 = (f32[512]{0:T(512)S(1)}, f32[512]{0:T(512)S(1)}, bf16[512,768]{1,0:T(8,128)(2,1)S(1)}) fusion(f32[768]{0:T(1024)S(1)} %get-tuple-element.8, f32[512,768]{1,0:T(8,128)} %get-tuple-element.10, f32[512,768]{1,0:T(8,128)} %get-tuple-element.9), kind=kLoop, calls=%fused_computation.21 | loop fusion | flops 9436160 | bytes 3939328 | tf_op jit(solution)/shard_map/reduce_sum | solution.py:82
  137.9 0.5 convolution_convert_fusion
  138.4 4.0 %fusion.6 = f32[32,4,3072]{2,0,1:T(8,128)S(1)} fusion(bf16[3072,768]{1,0:T(8,128)(2,1)} %param.9, bf16[32,4,768]{2,1,0:T(4,128)(2,1)S(1)} %convolution_convert_fusion), kind=kOutput, calls=%fused_computation.12 | convolution fusion | flops 603979776 | bytes 6488064 | tf_op jit(solution)/shard_map/th,dh->td/dot_general | solution.py:91
  142.4 2.2 copy.20
  144.7 0.6 dynamic-slice.1
  145.9 0.1 fusion.35
  146.1 0.1 stack.10
  146.1 0.1 stack.9
  146.2 69.6 %all-reduce.2 = f32[32,16,2]{1,0,2:T(8,128)S(1)} all-reduce(f32[32,16,2]{1,0,2:T(8,128)S(1)} %maximum_multiply_fusion), channel_id=3, replica_groups=mesh['noise'=8,'row'=16,'col'=2] {'row'}, use_global_device_ids=true, to_apply=%region_11.0.clone | all-reduce | flops 1024 | bytes 8192
  215.9 28.8 %all-reduce.8.cloned.1.call-done = f32[32,4,3072]{2,1,0:T(4,128)} async-done(((f32[32,4,3072]{2,1,0:T(4,128)}), f32[32,4,3072]{2,1,0:T(4,128)}) %all-reduce.8.cloned.1.call-update) | async-done | bytes 1572880
  244.7 1.4 fusion.9
  246.1 27.8 %all_gather.15 = f32[16,4,3072]{2,1,0:T(4,128)S(1)} all-gather(f32[2,4,3072]{2,1,0:T(4,128)S(1)} %fusion.9), channel_id=1, replica_groups=mesh['noise'=8,'row'=16,'col'=2] {'noise'}, dimensions={0}, use_global_device_ids=true | all-gather | bytes 884736 | tf_op jit(solution)/shard_map/all_gather | solution.py:107
  273.8 0.9 copy.32
  (33 shorter events, 0.3 us)
Async XLA Ops:
  6.5 33.3 %copy-start = (bf16[16,4,3072]{2,1,0:T(4,128)(2,1)S(1)}, bf16[16,4,3072]{2,1,0:T(4,128)(2,1)}, u32[]{:S(2)}) copy-start(bf16[16,4,3072]{2,1,0:T(4,128)(2,1)} %param.7) | copy-start | bytes 1179652
  6.5 89.3 %all-gather.2.cloned.1.call-start = ((), (), s32[]{:S(2)}) async-start(), calls=%async_computation.1 | async-start | bytes 3342336 | tf_op jit(solution)/shard_map/all_gather | solution.py:45
  26.5 108.2 %all-reduce.10.cloned.1.call-start = ((), (), s32[]{:S(2)}) async-start(), calls=%async_computation.3 | async-start | bytes 6291456 | tf_op jit(solution)/shard_map/psum | solution.py:79
  70.7 7.0 %copy-start.2 = (f32[3072]{0:T(1024)S(1)}, f32[3072]{0:T(1024)}, u32[]{:S(2)}) copy-start(f32[3072]{0:T(1024)} %param.8) | copy-start | bytes 36868
  77.7 14.3 %slice-start = ((s8[4718592]{0:T(1024)(128)(4,1)}), s8[524288]{0:T(1024)(128)(4,1)S(1)}, s32[]{:S(2)}) async-start(s8[4718592]{0:T(1024)(128)(4,1)} %bitcast.43), calls=%async_computation.4 | async-start | bytes 1048576
  84.7 7.3 %slice-start.1 = ((s8[4718592]{0:T(1024)(128)(4,1)}), s8[4194304]{0:T(1024)(128)(4,1)S(1)}, s32[]{:S(2)}) async-start(s8[4718592]{0:T(1024)(128)(4,1)} %bitcast.43), calls=%async_computation.5 | async-start | bytes 8388608
  95.8 7.3 %copy-start.3 = (s32[16,1]{0,1:T(1,128)S(1)}, s32[16,1]{0,1:T(1,128)}, u32[]{:S(2)}) copy-start(s32[16,1]{0,1:T(1,128)} %param.13) | copy-start | bytes 196
  102.9 141.7 %all-reduce.8.cloned.1.call-start = ((), (), s32[]{:S(2)}) async-start(), calls=%async_computation.2 | async-start | bytes 3145728
  138.3 6.3 %copy-start.4 = (u32[256]{0:T(256)S(1)}, u32[256]{0:T(256)}, u32[]{:S(2)}) copy-start(u32[256]{0:T(256)} %constant.75) | copy-start | bytes 3076
  138.4 106.3 %copy-start.1 = (bf16[2,16,3072]{2,1,0:T(8,128)(2,1)S(1)}, bf16[2,16,3072]{2,1,0:T(8,128)(2,1)}, u32[]{:S(2)}) copy-start(bf16[2,16,3072]{2,1,0:T(8,128)(2,1)} %all_to_all.16) | copy-start | bytes 589828
Sparse Core Ops, SparseCore 0:
  26.6 49.4 all-gather.1
  103.0 31.6 all-reduce.9
  144.8 99.8 all-reduce.7
where the time goes:
time: 282 us; the launch traced here: 281 us
  blocking collectives  159 us (56%)
  waiting for transfers between devices  60.4 us (21%)
  matrix products  22.1 us (8%)
  other arithmetic  17.7 us (6%)
  between operations  14.6 us (5%)
  local copies, waits for them, and re-layouts  7.19 us (3%)
    unnamed x2, blocking collectives  79.7 us
    psum x1, waiting for transfers between devices, body(): preact, back_grad, ug = lax.psum((preact_part, back_part, ug_part), 'col')  31.5 us
    unnamed x4, waiting for transfers between devices  28.8 us
    all_gather x1, blocking collectives, body(): return lax.all_gather(total, 'noise', axis=0, tiled=True)  27.8 us
    all_gather x1, blocking collectives, body(): plane_images = lax.all_gather(own_images, 'row', axis=0, tiled=True)  25.4 us
    all_to_all x1, blocking collectives, body(): lax.all_to_all(cotangent, 'noise', split_axis=0, concat_axis=1, tiled=True)  19.1 us
    convert_element_type x1, other arithmetic, body(): scaled = (normed * gain).astype(jnp.bfloat16)  7.28 us
    dot_general x1, matrix products, body(): jnp.einsum('td,hd->th', plane_cot.reshape(n, width_local), down_weight, p...  7.09 us
  transfers between devices with their start and end apart: 3, of which 2 were waited for; matrix products, arithmetic and copies ran while one was open for 10% of the time, Pallas kernels for 0%

commit v1 on v0

--- a/solution.py
+++ b/solution.py
@@ -41,8 +41,11 @@
     slots = all_seeds.shape[0]
     own_cot = lax.all_to_all(cotangent, "noise", split_axis=0, concat_axis=1, tiled=True)
     own_images = lax.dynamic_slice_in_dim(images, noise_index * part, part)
-    plane_images = lax.all_gather(own_images, "row", axis=0, tiled=True)
-    plane_cot = lax.all_gather(own_cot, "row", axis=0, tiled=True)
+    plane_images, plane_cot = jnp.split(
+        lax.all_gather(jnp.concatenate([own_images, own_cot], axis=1), "row", axis=0, tiled=True),
+        [own_images.shape[1]],
+        axis=1,
+    )
     image_ids = jnp.arange(image_count, dtype=jnp.int32)
     onehot = (assign[:, 0][:, None] == image_ids[None, :]).astype(jnp.float32)
     counts = jnp.sum(onehot, axis=0)

time: 282 us -> 297 us (1.053)
  waiting for transfers between devices: 60.4 us -> 112 us
  blocking collectives: 159 us -> 115 us
  starting transfers between devices: 0.27 us -> 8.72 us
    all_gather x1, waiting for transfers between devices: 0.01 us -> 38.7 us  [body(): lax.all_gather(jnp.concatenate([own_images, own_cot], axis=1), 'row', axi...]
    all_gather x1 -> x0, blocking collectives: 25.4 us -> none  [body(): plane_images = lax.all_gather(own_images, 'row', axis=0, tiled=True)]
    all_to_all x1 -> x0, blocking collectives: 19.1 us -> none  [body(): lax.all_to_all(cotangent, 'noise', split_axis=0, concat_axis=1, tiled=True)]
    all_to_all x0 -> x1, waiting for transfers between devices: none -> 10.4 us  [body(): lax.all_to_all(cotangent, 'noise', split_axis=0, concat_axis=1, tiled=True)]
    all_to_all x0 -> x1, starting transfers between devices: none -> 8.6 us  [body(): lax.all_to_all(cotangent, 'noise', split_axis=0, concat_axis=1, tiled=True)]
    dot_general x1, matrix products: 7.09 us -> 3.79 us  [body(): jnp.einsum('td,hd->th', plane_cot.reshape(n, width_local), down_weight, p...]
  transfers between devices with their start and end apart: 3 -> 4, of which waited for: 2 -> 4; matrix products, arithmetic and copies ran while one was open for 10% -> 2% of each run, Pallas kernels for 0% -> 0%
where the time goes in v1:
time: 297 us
  blocking collectives  115 us (39%)
  waiting for transfers between devices  112 us (38%)
  matrix products  20.2 us (7%)
  other arithmetic  18.9 us (6%)
  between operations  14.7 us (5%)
  starting transfers between devices  8.72 us (3%)
  local copies, waits for them, and re-layouts  7.85 us (3%)
    unnamed x2, blocking collectives  79.7 us
    all_gather x1, waiting for transfers between devices, body(): lax.all_gather(jnp.concatenate([own_images, own_cot], axis=1), 'row', axi...  38.7 us
    psum x1, waiting for transfers between devices, body(): preact, back_grad, ug = lax.psum((preact_part, back_part, ug_part), 'col')  33.9 us
    unnamed x4, waiting for transfers between devices  29 us
    all_gather x1, blocking collectives, body(): return lax.all_gather(total, 'noise', axis=0, tiled=True)  27.8 us
    all_to_all x1, waiting for transfers between devices, body(): lax.all_to_all(cotangent, 'noise', split_axis=0, concat_axis=1, tiled=True)  10.4 us
    all_to_all x1, starting transfers between devices, body(): lax.all_to_all(cotangent, 'noise', split_axis=0, concat_axis=1, tiled=True)  8.6 us
    convert_element_type x1, other arithmetic, body(): scaled = (normed * gain).astype(jnp.bfloat16)  7.68 us
  transfers between devices with their start and end apart: 4, of which 4 were waited for; matrix products, arithmetic and copies ran while one was open for 2% of the time, Pallas kernels for 0%

profile of v1, /device:TPU:2, one launch (start us, length us, event | category | flops | bytes accessed | tf_op | source)
XLA Modules:
  0.0 297.0 jit_solution(16835909474732585543)
XLA Ops:
  6.5 8.6 %all-to-all-start = ((bf16[16,2,3072]{2,1,0:T(2,128)(2,1)}), bf16[16,2,3072]{2,1,0:T(2,128)(2,1)S(1)}, u32[]{:S(2)}, u32[]{:S(2)}) async-start(bf16[16,2,3072]{2,1,0:T(2,128)(2,1)} %param.11), calls=%async_computation | async-start | bytes 393216 | tf_op jit(solution)/shard_map/all_to_all | solution.py:42
  15.2 10.4 %all-to-all-done = bf16[16,2,3072]{2,1,0:T(2,128)(2,1)S(1)} async-done(((bf16[16,2,3072]{2,1,0:T(2,128)(2,1)}), bf16[16,2,3072]{2,1,0:T(2,128)(2,1)S(1)}, u32[]{:S(2)}, u32[]{:S(2)}) %all-to-all-start) | async-done | bytes 196640 | tf_op jit(solution)/shard_map/all_to_all | solution.py:42
  25.6 0.1 copy.26
  25.8 0.8 pad_maximum_fusion
  26.8 0.1 mul.175
  26.9 1.3 dynamic-slice
  28.9 0.9 dynamic-update-slice
  29.8 10.1 %all-reduce = s32[16]{0:T(128)S(1)} all-reduce(s32[16]{0:T(128)S(1)} %dynamic-update-slice), channel_id=1, replica_groups=mesh['noise'=8,'row'=16,'col'=2] {'noise'}, use_global_device_ids=true, to_apply=%add | all-reduce | flops 16 | bytes 128
  39.9 3.4 %multiply_reduce_fusion = f32[768]{0:T(1024)S(1)} fusion(bf16[3072,768]{1,0:T(8,128)(2,1)} %param.9, f32[3072]{0:T(1024)} %param.8), kind=kLoop, calls=%fused_computation.2 | loop fusion | flops 7077120 | bytes 4733952 | tf_op jit(solution)/shard_map/reduce_sum | solution.py:81
  43.3 0.1 add_multiply_fusion
  43.4 38.7 %all-gather.2.cloned.1.call-done = bf16[32,20,3072]{2,1,0:T(8,128)(2,1)} async-done(((bf16[2,20,3072]{2,1,0:T(8,128)(2,1)}), bf16[32,20,3072]{2,1,0:T(8,128)(2,1)}) %all-gather.2.cloned.1.call-update) | async-done | bytes 3932176 | tf_op jit(solution)/shard_map/all_gather | solution.py:45
  82.2 6.8 %fusion.45 = (f32[32,16]{1,0:T(8,128)S(1)}, f32[32,16,3072]{2,1,0:T(8,128)}) fusion(s32[16]{0:T(128)S(1)} %broadcast_multiply_fusion.1, s32[32,3072]{1,0:T(8,128)S(1)} %add_multiply_fusion, s32[16]{0:T(128)S(1)} %bitcast.51, bf16[32,20,3072]{2,1,0:T(8,128)(2,1)} %all-gather.2.cloned.1.call-done), kind=kOutput, calls=%fused_computation.70 | convolution fusion | flops 31456960 | bytes 7473280 | tf_op jit(solution)/shard_map/si,tid->tsd/dot_general | solution.py:52
  89.0 3.5 %psum.35 = f32[32,16]{1,0:T(8,128)S(1)} all-reduce(f32[32,16]{1,0:T(8,128)S(1)} %get-tuple-element.18), channel_id=1, replica_groups=mesh['noise'=8,'row'=16,'col'=2] {'col'}, use_global_device_ids=true, to_apply=%region_1.0 | all-reduce | flops 512 | bytes 4096 | tf_op jit(solution)/shard_map/psum | solution.py:65
  92.5 3.6 %multiply_reduce_fusion.1 = f32[32,16]{1,0:T(8,128)S(1)} fusion(f32[32,16,3072]{2,1,0:T(8,128)} %get-tuple-element.19, f32[32,16]{1,0:T(8,128)S(1)} %broadcast_multiply_fusion), kind=kLoop, calls=%fused_computation.10 | loop fusion | flops 4718080 | bytes 6295552 | tf_op jit(solution)/shard_map/reduce_sum | solution.py:67
  96.1 3.7 %all-reduce.3 = (f32[32,16]{1,0:T(8,128)S(1)}, f32[768]{0:T(1024)S(1)}) all-reduce(f32[32,16]{1,0:T(8,128)S(1)} %multiply_reduce_fusion.1, f32[768]{0:T(1024)S(1)} %multiply_reduce_fusion), channel_id=1, replica_groups=mesh['noise'=8,'row'=16,'col'=2] {'col'}, use_global_device_ids=true, to_apply=%region_3.0 | all-reduce | flops 1280 | bytes 10240 | tf_op jit(solution)/shard_map/psum | solution.py:67
  99.9 7.7 %multiply_convert_fusion = (bf16[32,16,3072]{2,1,0:T(8,128)(2,1)S(1)}, f32[32,16,3072]{2,1,0:T(8,128)}) fusion(f32[3072]{0:T(1024)S(1)} %copy-done.1, f32[32,16]{1,0:T(8,128)S(1)} %get-tuple-element.17, f32[32,16,3072]{2,1,0:T(8,128)} %get-tuple-element.19, f32[32,16]{1,0:T(8,128)S(1)} %broadcast_multiply_fusion), kind=kLoop, calls=%fused_computation.9 | loop fusion | flops 6291456 | bytes 15745024 | tf_op jit(solution)/shard_map/convert_element_type | solution.py:70
  107.6 3.8 %fusion.47 = f32[512,768]{1,0:T(8,128)} fusion(bf16[512,3072]{1,0:T(8,128)(2,1)S(1)} %bitcast.46, bf16[3072,768]{1,0:T(8,128)(2,1)S(1)} %bitcast.43), kind=kOutput, calls=%fused_computation.72 | convolution fusion | flops 2415919104 | bytes 9437184 | tf_op jit(solution)/shard_map/dot_general | solution.py:72
  111.3 1.4 split.9
  112.7 3.8 %fusion.46 = f32[512,768]{1,0:T(8,128)} fusion(bf16[512,3072]{1,0:T(8,128)(2,1)S(1)} %bitcast.44, bf16[768,3072]{1,0:T(8,128)(2,1)S(1)} %bitcast.56), kind=kOutput, calls=%fused_computation.71 | convolution fusion | flops 2415919104 | bytes 9437184 | tf_op jit(solution)/shard_map/td,hd->th/dot_general | solution.py:75
  116.6 33.9 %all-reduce.10.cloned.1.call-done = (f32[512,768]{1,0:T(8,128)}, f32[512,768]{1,0:T(8,128)}) async-done(((f32[512,768]{1,0:T(8,128)}, f32[512,768]{1,0:T(8,128)}), (f32[512,768]{1,0:T(8,128)}, f32[512,768]{1,0:T(8,128)})) %all-reduce.10.cloned.1.call-update) | async-done | bytes 3145744 | tf_op jit(solution)/shard_map/psum | solution.py:82
  150.5 3.2 %fusion.10 = (f32[512]{0:T(512)S(1)}, f32[512]{0:T(512)S(1)}, bf16[512,768]{1,0:T(8,128)(2,1)S(1)}) fusion(f32[768]{0:T(1024)S(1)} %get-tuple-element.8, f32[512,768]{1,0:T(8,128)} %get-tuple-element.10, f32[512,768]{1,0:T(8,128)} %get-tuple-element.9), kind=kLoop, calls=%fused_computation.21 | loop fusion | flops 9436160 | bytes 3939328 | tf_op jit(solution)/shard_map/reduce_sum | solution.py:85
  153.7 0.5 convolution_convert_fusion
  154.1 4.0 %fusion.6 = f32[32,4,3072]{2,0,1:T(8,128)S(1)} fusion(bf16[3072,768]{1,0:T(8,128)(2,1)} %param.9, bf16[32,4,768]{2,1,0:T(4,128)(2,1)S(1)} %convolution_convert_fusion), kind=kOutput, calls=%fused_computation.12 | convolution fusion | flops 603979776 | bytes 6488064 | tf_op jit(solution)/shard_map/th,dh->td/dot_general | solution.py:94
  158.1 2.2 copy.20
  160.4 0.6 dynamic-slice.1
  161.6 0.1 fusion.36
  161.8 0.1 stack.9
  161.9 69.5 %all-reduce.2 = f32[32,16,2]{1,0,2:T(8,128)S(1)} all-reduce(f32[32,16,2]{1,0,2:T(8,128)S(1)} %maximum_multiply_fusion), channel_id=3, replica_groups=mesh['noise'=8,'row'=16,'col'=2] {'row'}, use_global_device_ids=true, to_apply=%region_11.0.clone | all-reduce | flops 1024 | bytes 8192
  231.5 29.0 %all-reduce.8.cloned.1.call-done = f32[32,4,3072]{2,1,0:T(4,128)} async-done(((f32[32,4,3072]{2,1,0:T(4,128)}), f32[32,4,3072]{2,1,0:T(4,128)}) %all-reduce.8.cloned.1.call-update) | async-done | bytes 1572880
  260.4 1.4 fusion.9
  261.8 27.8 %all_gather.11 = f32[16,4,3072]{2,1,0:T(4,128)S(1)} all-gather(f32[2,4,3072]{2,1,0:T(4,128)S(1)} %fusion.9), channel_id=1, replica_groups=mesh['noise'=8,'row'=16,'col'=2] {'noise'}, dimensions={0}, use_global_device_ids=true | all-gather | bytes 884736 | tf_op jit(solution)/shard_map/all_gather | solution.py:110
  289.6 0.9 copy.32
  (43 shorter events, 0.5 us)
Async XLA Ops:
  6.5 8.7 %copy-start = (bf16[16,4,3072]{2,1,0:T(4,128)(2,1)S(1)}, bf16[16,4,3072]{2,1,0:T(4,128)(2,1)}, u32[]{:S(2)}) copy-start(bf16[16,4,3072]{2,1,0:T(4,128)(2,1)} %param.7) | copy-start | bytes 1179652
  6.5 75.6 %copy-start.2 = (s32[16,1]{0,1:T(1,128)S(1)}, s32[16,1]{0,1:T(1,128)}, u32[]{:S(2)}) copy-start(s32[16,1]{0,1:T(1,128)} %param.13) | copy-start | bytes 196
  6.5 19.1 %all-to-all-start = ((bf16[16,2,3072]{2,1,0:T(2,128)(2,1)}), bf16[16,2,3072]{2,1,0:T(2,128)(2,1)S(1)}, u32[]{:S(2)}, u32[]{:S(2)}) async-start(bf16[16,2,3072]{2,1,0:T(2,128)(2,1)} %param.11), calls=%async_computation | async-start | bytes 393216 | tf_op jit(solution)/shard_map/all_to_all | solution.py:42
  15.1 67.0 %all-gather.2.cloned.1.call-start = ((), (), s32[]{:S(2)}) async-start(), calls=%async_computation.1 | async-start | bytes 5013504 | tf_op jit(solution)/shard_map/all_gather | solution.py:45
  26.7 123.8 %all-reduce.10.cloned.1.call-start = ((), (), s32[]{:S(2)}) async-start(), calls=%async_computation.3 | async-start | bytes 6291456 | tf_op jit(solution)/shard_map/psum | solution.py:82
  89.0 10.8 %copy-start.1 = (f32[3072]{0:T(1024)S(1)}, f32[3072]{0:T(1024)}, u32[]{:S(2)}) copy-start(f32[3072]{0:T(1024)} %param.8) | copy-start | bytes 36868
  92.5 15.1 %slice-start = ((s8[4718592]{0:T(1024)(128)(4,1)}), s8[524288]{0:T(1024)(128)(4,1)S(1)}, s32[]{:S(2)}) async-start(s8[4718592]{0:T(1024)(128)(4,1)} %bitcast.42), calls=%async_computation.4 | async-start | bytes 1048576
  99.8 7.7 %slice-start.1 = ((s8[4718592]{0:T(1024)(128)(4,1)}), s8[4194304]{0:T(1024)(128)(4,1)S(1)}, s32[]{:S(2)}) async-start(s8[4718592]{0:T(1024)(128)(4,1)} %bitcast.42), calls=%async_computation.5 | async-start | bytes 8388608
  99.8 11.5 %slice-start.2 = ((s8[4718592]{0:T(1024)(128)(4,1)}), s8[4194304]{0:T(1024)(128)(4,1)S(1)}, s32[]{:S(2)}) async-start(s8[4718592]{0:T(1024)(128)(4,1)} %bitcast.47), calls=%async_computation.6 | async-start | bytes 8388608
  99.8 12.9 %slice-start.4 = ((s8[4718592]{0:T(1024)(128)(4,1)}), s8[4194304]{0:T(1024)(128)(4,1)S(1)}, s32[]{:S(2)}) async-start(s8[4718592]{0:T(1024)(128)(4,1)} %bitcast.55), calls=%async_computation.8 | async-start | bytes 8388608
  107.5 3.8 %slice-start.3 = ((s8[4718592]{0:T(1024)(128)(4,1)}), s8[524288]{0:T(1024)(128)(4,1)S(1)}, s32[]{:S(2)}) async-start(s8[4718592]{0:T(1024)(128)(4,1)} %bitcast.47), calls=%async_computation.7 | async-start | bytes 1048576
  107.5 5.2 %slice-start.5 = ((s8[4718592]{0:T(1024)(128)(4,1)}), s8[524288]{0:T(1024)(128)(4,1)S(1)}, s32[]{:S(2)}) async-start(s8[4718592]{0:T(1024)(128)(4,1)} %bitcast.55), calls=%async_computation.9 | async-start | bytes 1048576
  116.6 143.9 %all-reduce.8.cloned.1.call-start = ((), (), s32[]{:S(2)}) async-start(), calls=%async_computation.2 | async-start | bytes 3145728
  154.1 6.3 %copy-start.3 = (u32[256]{0:T(256)S(1)}, u32[256]{0:T(256)}, u32[]{:S(2)}) copy-start(u32[256]{0:T(256)} %constant.75) | copy-start | bytes 3076
Sparse Core Ops, SparseCore 0:
  26.8 55.3 all-gather.1
  116.7 33.7 all-reduce.9
  160.5 99.8 all-reduce.7
